TPU v7x, 32 devices: a whole 2x2x4 slice. The times are simulated.
32 devices in a mesh: dp: 2 (over x), row: 4 (over y, core), col: 4 (over z).
Axes of the slice: x: 2, y: 2, z: 4, core: 2. Of those that a mesh axis runs over, the one named last changes fastest.
Arguments:
- tokens: bfloat16 [512, 6144], P(('dp', 'col'), 'row'), may hold values from -6 to 6
- grad_out: bfloat16 [512, 6144], P(('dp', 'col'), 'row'), may hold values from -6 to 6
- w_in: bfloat16 [6144, 24576], P('row', 'col'), may hold values from -0.078125 to 0.078125
- w_out: bfloat16 [24576, 6144], P('col', 'row'), may hold values from -0.0390625 to 0.0390625
Outputs:
- output: bfloat16 [512, 6144], P(('dp', 'col'), 'row')
- grad_tokens: bfloat16 [512, 6144], P(('dp', 'col'), 'row')
- grad_w_in: bfloat16 [6144, 24576], P('row', 'col')
- grad_w_out: bfloat16 [24576, 6144], P('col', 'row')
All inputs are finite; a program needn't handle non-finite values.
Results may differ from a plain program's by a relative error of at most 0.03.
Values may be sent and summed in bfloat16 or wider, within the bound.
A program may use at most 192 MiB of HBM per device.

v0:
```python
import jax
import jax.numpy as jnp
from jax import lax
from jax.sharding import PartitionSpec as P


def gelu_tanh(value):
    return jax.nn.gelu(value, approximate=True)


def gelu_back(pre, grad_hidden):
    _, pullback = jax.vjp(gelu_tanh, pre)
    return pullback(grad_hidden)[0].astype(jnp.bfloat16)


def contract_rows(left, right):
    return lax.dot_general(
        left, right, (((0,), (0,)), ((), ())), preferred_element_type=jnp.float32
    )


def contract_cols(left, right):
    return lax.dot_general(
        left, right, (((1,), (1,)), ((), ())), preferred_element_type=jnp.float32
    )


def shards(tokens, grad_out, w_in, w_out):
    group_x, group_dy = (
        lax.all_gather(tokens, "col", axis=0, tiled=True),
        lax.all_gather(grad_out, "col", axis=0, tiled=True),
    )
    pre_part = jnp.dot(group_x, w_in, preferred_element_type=jnp.float32)
    grad_part = contract_cols(group_dy, w_out)
    pre_share, grad_share = (
        lax.psum_scatter(
            pre_part.astype(jnp.bfloat16), "row", scatter_dimension=0, tiled=True
        ).astype(jnp.float32),
        lax.psum_scatter(
            grad_part.astype(jnp.bfloat16), "row", scatter_dimension=0, tiled=True
        ).astype(jnp.float32),
    )
    hidden_share = gelu_tanh(pre_share).astype(jnp.bfloat16)
    grad_pre_share = gelu_back(pre_share, grad_share)
    hidden, grad_pre = (
        lax.all_gather(hidden_share, "row", axis=0, tiled=True),
        lax.all_gather(grad_pre_share, "row", axis=0, tiled=True),
    )
    out_part = jnp.dot(hidden, w_out, preferred_element_type=jnp.float32)
    back_part = contract_cols(grad_pre, w_in)
    output, grad_tokens = (
        lax.psum_scatter(
            out_part.astype(jnp.bfloat16), "col", scatter_dimension=0, tiled=True
        ).astype(jnp.float32),
        lax.psum_scatter(
            back_part.astype(jnp.bfloat16), "col", scatter_dimension=0, tiled=True
        ).astype(jnp.float32),
    )
    local_in = contract_rows(group_x, grad_pre)
    local_out = contract_rows(hidden, group_dy)
    total_in, total_out = (
        lax.psum(local_in.astype(jnp.bfloat16), "dp").astype(jnp.float32),
        lax.psum(local_out.astype(jnp.bfloat16), "dp").astype(jnp.float32),
    )
    return (
        output.astype(jnp.bfloat16),
        grad_tokens.astype(jnp.bfloat16),
        total_in.astype(jnp.bfloat16),
        total_out.astype(jnp.bfloat16),
    )


def solution(mesh):
    return jax.shard_map(
        shards,
        mesh=mesh,
        in_specs=(
            P(("dp", "col"), "row"),
            P(("dp", "col"), "row"),
            P("row", "col"),
            P("col", "row"),
        ),
        out_specs=(
            P(("dp", "col"), "row"),
            P(("dp", "col"), "row"),
            P("row", "col"),
            P("col", "row"),
        ),
        check_vma=False,
    )
```

profile of v0, /device:TPU:0, one launch (start us, length us, event | category | flops | bytes accessed | tf_op | source)
XLA Modules:
  0.0 1098.7 jit_solution(2183926351523319601)
XLA Ops:
  7.2 0.0 reduce-scatter.9.cloned.1.call-start
  7.2 21.5 %all_gather.14 = bf16[256,1536]{1,0:T(8,128)(2,1)S(1)} all-gather(bf16[64,1536]{1,0:T(8,128)(2,1)} %param.5), channel_id=1, replica_groups=mesh['dp'=2,'row'=4,'col'=4] {'col'}, dimensions={0}, use_global_device_ids=true | all-gather | bytes 983040 | tf_op jit(solution)/shard_map/all_gather | solution.py:31
  28.7 10.1 convolution_convert_fusion.2
  38.9 0.0 reduce-scatter.9.cloned.1.call-update
  38.9 0.0 reduce-scatter.5.cloned.1.call-start
  38.9 0.9 copy-done.1
  39.8 17.7 %all_gather.12 = bf16[256,1536]{1,0:T(8,128)(2,1)S(1)} all-gather(bf16[64,1536]{1,0:T(8,128)(2,1)S(1)} %copy-done.1), channel_id=1, replica_groups=mesh['dp'=2,'row'=4,'col'=4] {'col'}, dimensions={0}, use_global_device_ids=true | all-gather | bytes 983040 | tf_op jit(solution)/shard_map/all_gather | solution.py:30
  57.5 12.8 %convolution_convert_fusion.3 = bf16[256,6144]{1,0:T(8,128)(2,1)} fusion(bf16[256,1536]{1,0:T(8,128)(2,1)S(1)} %all_gather.12, bf16[1536,6144]{1,0:T(8,128)(2,1)} %param.6), kind=kOutput, calls=%fused_computation.4 | convolution fusion | flops 4833411072 | bytes 22806528 | tf_op jit(solution)/shard_map/dot_general | solution.py:33
  70.2 0.0 reduce-scatter.5.cloned.1.call-update
  70.3 0.0 all-gather.5.cloned.1.call-start
  70.3 6.0 reduce-scatter.9.cloned.1.call-done
  76.4 41.3 %reduce-scatter.5.cloned.1.call-done = bf16[64,6144]{1,0:T(8,128)(2,1)} async-done(((bf16[256,6144]{1,0:T(8,128)(2,1)}), bf16[64,6144]{1,0:T(8,128)(2,1)}) %reduce-scatter.5.cloned.1.call-update) | async-done | bytes 786448 | tf_op jit(solution)/shard_map/reduce_scatter | solution.py:36
  117.6 3.7 fusion.4
  121.3 0.0 all-gather.5.cloned.1.call-update
  121.4 0.0 all-gather.3.cloned.1.call-start
  121.4 0.5 all-gather.3.cloned.1.call-update
  121.9 0.2 all-reduce.3.cloned.1.call-start
  122.2 27.9 %all-gather.5.cloned.1.call-done = bf16[256,6144]{1,0:T(8,128)(2,1)} async-done(((bf16[64,6144]{1,0:T(8,128)(2,1)}), bf16[256,6144]{1,0:T(8,128)(2,1)}) %all-gather.5.cloned.1.call-update) | async-done | bytes 3145744 | tf_op jit(solution)/shard_map/all_gather | solution.py:47
  150.0 11.6 %fusion = bf16[1536,6144]{0,1:T(8,128)(2,1)} fusion(bf16[256,6144]{1,0:T(8,128)(2,1)} %all-gather.5.cloned.1.call-done, bf16[256,1536]{1,0:T(8,128)(2,1)S(1)} %all_gather.12), kind=kOutput, calls=%fused_computation.2 | convolution fusion | flops 4841275392 | bytes 22806528 | tf_op jit(solution)/shard_map/dot_general | solution.py:17
  161.7 19.0 %all-gather.3.cloned.1.call-done = bf16[256,6144]{1,0:T(8,128)(2,1)} async-done(((bf16[64,6144]{1,0:T(8,128)(2,1)}), bf16[256,6144]{1,0:T(8,128)(2,1)}) %all-gather.3.cloned.1.call-update) | async-done | bytes 3145744 | tf_op jit(solution)/shard_map/all_gather | solution.py:46
  180.6 11.4 %convolution_convert_fusion = bf16[6144,1536]{1,0:T(8,128)(2,1)} fusion(bf16[256,6144]{1,0:T(8,128)(2,1)} %all-gather.3.cloned.1.call-done, bf16[256,1536]{1,0:T(8,128)(2,1)S(1)} %all_gather.14), kind=kOutput, calls=%fused_computation | convolution fusion | flops 4841275392 | bytes 22806528 | tf_op jit(solution)/shard_map/dot_general | solution.py:17
  192.0 0.0 all-reduce.3.cloned.1.call-update
  192.1 0.0 reduce-scatter.7.cloned.1.call-start
  192.1 12.2 %convolution_convert_fusion.5 = bf16[256,1536]{1,0:T(8,128)(2,1)} fusion(bf16[256,6144]{1,0:T(8,128)(2,1)} %all-gather.3.cloned.1.call-done, bf16[6144,1536]{1,0:T(8,128)(2,1)} %param.7), kind=kOutput, calls=%fused_computation.11 | convolution fusion | flops 4832231424 | bytes 22806528 | tf_op jit(solution)/shard_map/dot_general | solution.py:49
  204.3 0.0 reduce-scatter.7.cloned.1.call-update
  204.3 0.0 reduce-scatter.11.cloned.1.call-start
  204.4 9.9 convolution_convert_fusion.4
  214.4 807.1 %all-reduce.3.cloned.1.call-done = (bf16[1536,6144]{0,1:T(8,128)(2,1)}, bf16[6144,1536]{1,0:T(8,128)(2,1)}) async-done(((bf16[1536,6144]{0,1:T(8,128)(2,1)}, bf16[6144,1536]{1,0:T(8,128)(2,1)}), (bf16[1536,6144]{0,1:T(8,128)(2,1)}, bf16[6144,1536]{1,0:T(8,128)(2,1)})) %all-reduce.3.cloned.1.call-update) | async-done | bytes 37748752 | tf_op jit(solution)/shard_map/psum | solution.py:62
  1021.5 24.6 %copy.8 = bf16[1536,6144]{1,0:T(8,128)(2,1)} copy(bf16[1536,6144]{0,1:T(8,128)(2,1)} %get-tuple-element.8) | data formatting | bytes 37748736
  1046.1 3.6 reduce-scatter.7.cloned.1.call-done
  1049.8 25.6 %reduce-scatter.11.cloned.1.call-done = bf16[64,1536]{1,0:T(8,128)(2,1)} async-done(((bf16[256,1536]{1,0:T(8,128)(2,1)}), bf16[64,1536]{1,0:T(8,128)(2,1)}) %reduce-scatter.11.cloned.1.call-update) | async-done | bytes 196624 | tf_op jit(solution)/shard_map/reduce_scatter | solution.py:55
  1075.4 16.5 %copy.11 = bf16[6144,1536]{1,0:T(8,128)(2,1)} copy(bf16[6144,1536]{1,0:T(8,128)(2,1)} %get-tuple-element.15) | data formatting | bytes 37748736
  (4 shorter events, 0.0 us)
Async XLA Ops:
  7.2 69.2 %reduce-scatter.9.cloned.1.call-start = ((), (), s32[]{:S(2)}) async-start(), calls=%async_computation.7 | async-start | bytes 3932160 | tf_op jit(solution)/shard_map/reduce_scatter | solution.py:39
  38.9 0.9 copy-start.1
  38.9 78.7 %reduce-scatter.5.cloned.1.call-start = ((), (), s32[]{:S(2)}) async-start(), calls=%async_computation.4 | async-start | bytes 3932160 | tf_op jit(solution)/shard_map/reduce_scatter | solution.py:36
  70.3 79.8 %all-gather.5.cloned.1.call-start = ((), (), s32[]{:S(2)}) async-start(), calls=%async_computation.8 | async-start | bytes 3932160 | tf_op jit(solution)/shard_map/all_gather | solution.py:47
  121.4 59.2 %all-gather.3.cloned.1.call-start = ((), (), s32[]{:S(2)}) async-start(), calls=%async_computation.5 | async-start | bytes 3932160 | tf_op jit(solution)/shard_map/all_gather | solution.py:46
  121.9 899.6 %all-reduce.3.cloned.1.call-start = ((), (), s32[]{:S(2)}) async-start(), calls=%async_computation.10 | async-start | bytes 75497472 | tf_op jit(solution)/shard_map/psum | solution.py:62
  192.1 12.3 %copy-start = (bf16[256,6144]{1,0:T(8,128)(2,1)S(1)}, bf16[256,6144]{1,0:T(8,128)(2,1)}, u32[]{:S(2)}) copy-start(bf16[256,6144]{1,0:T(8,128)(2,1)} %all-gather.5.cloned.1.call-done) | copy-start | bytes 9437188
  192.1 857.7 %reduce-scatter.7.cloned.1.call-start = ((), (), s32[]{:S(2)}) async-start(), calls=%async_computation.6 | async-start | bytes 983040 | tf_op jit(solution)/shard_map/reduce_scatter | solution.py:52
  204.3 871.0 %reduce-scatter.11.cloned.1.call-start = ((), (), s32[]{:S(2)}) async-start(), calls=%async_computation.9 | async-start | bytes 983040 | tf_op jit(solution)/shard_map/reduce_scatter | solution.py:55
Sparse Core Ops, SparseCore 0:
  39.0 37.3 reduce-scatter.8
  79.6 37.9 reduce-scatter.4
  121.5 28.5 all-gather.4
  152.0 28.5 all-gather.2
  192.2 829.2 all-reduce.2
  1024.4 25.3 reduce-scatter.6
  1052.8 22.5 reduce-scatter.10
where the time goes:
time: 1100 us
  waiting for transfers between devices  931 us (85%)
  matrix products  68.1 us (6%)
  local copies, waits for them, and re-layouts  41.9 us (4%)
  blocking collectives  39.2 us (4%)
  between operations  14.1 us (1%)
    psum x1, waiting for transfers between devices, shards(): lax.psum(local_in.astype(jnp.bfloat16), 'dp').astype(jnp.float32)  807 us
    unnamed x6, local copies, waits for them, and re-layouts  41.9 us
    reduce_scatter x1, waiting for transfers between devices, shards(): lax.psum_scatter(pre_part.astype(jnp.bfloat16), 'row', scatter_dimension=...  41.3 us
    all_gather x1, waiting for transfers between devices, shards(): lax.all_gather(grad_pre_share, 'row', axis=0, tiled=True)  27.9 us
    reduce_scatter x1, waiting for transfers between devices, shards(): lax.psum_scatter(back_part.astype(jnp.bfloat16), 'col', scatter_dimension...  25.6 us
    dot_general x2, matrix products, contract_rows(): lax.dot_general(left, right, (((0,), (0,)), ((), ())), preferred_element_...  23 us
  transfers between devices with their start and end apart: 7, of which 7 were waited for; matrix products, arithmetic and copies ran while one was open for 6% of the time, Pallas kernels for 0%

commit v1 on v0

v1 whole, which is shorter than its diff:
```python
import jax
import jax.numpy as jnp
from jax import lax
from jax.sharding import PartitionSpec as P


def gelu_tanh(value):
    return jax.nn.gelu(value, approximate=True)


def gelu_back(pre, grad_hidden):
    _, pullback = jax.vjp(gelu_tanh, pre)
    return pullback(grad_hidden)[0].astype(jnp.bfloat16)


def contract_rows(left, right):
    return lax.dot_general(
        left, right, (((0,), (0,)), ((), ())), preferred_element_type=jnp.float32
    )


def contract_cols(left, right):
    return lax.dot_general(
        left, right, (((1,), (1,)), ((), ())), preferred_element_type=jnp.float32
    )


def gather(value, axis):
    return lax.all_gather(value, axis, axis=0, tiled=True)


def swap(value):
    return lax.ppermute(value, "dp", [(0, 1), (1, 0)])


def scatter(value, axis):
    return lax.psum_scatter(value, axis, scatter_dimension=0, tiled=True)


def shards(tokens, grad_out, w_in, w_out):
    group_x, group_dy = gather(tokens, "col"), gather(grad_out, "col")
    other_x, other_dy = swap(group_x), swap(group_dy)
    pre_part = jnp.dot(group_x, w_in, preferred_element_type=jnp.float32)
    pre_share = scatter(pre_part.astype(jnp.bfloat16), "row").astype(jnp.float32)
    grad_part = contract_cols(group_dy, w_out)
    grad_share = scatter(grad_part.astype(jnp.bfloat16), "row").astype(jnp.float32)
    hidden_share = gelu_tanh(pre_share).astype(jnp.bfloat16)
    grad_pre_share = gelu_back(pre_share, grad_share)
    hidden, grad_pre = gather(hidden_share, "row"), gather(grad_pre_share, "row")
    other_hidden = gather(swap(hidden_share), "row")
    other_grad_pre = gather(swap(grad_pre_share), "row")
    out_part = jnp.dot(hidden, w_out, preferred_element_type=jnp.float32)
    output = scatter(out_part.astype(jnp.bfloat16), "col")
    back_part = contract_cols(grad_pre, w_in)
    grad_tokens = scatter(back_part.astype(jnp.bfloat16), "col")
    both_x = jnp.concatenate([group_x, other_x], axis=0)
    both_dy = jnp.concatenate([group_dy, other_dy], axis=0)
    both_hidden = jnp.concatenate([hidden, other_hidden], axis=0)
    both_grad_pre = jnp.concatenate([grad_pre, other_grad_pre], axis=0)
    total_out = contract_rows(both_hidden, both_dy).astype(jnp.bfloat16)
    total_in = contract_rows(both_x, both_grad_pre).astype(jnp.bfloat16)
    return output, grad_tokens, total_in, total_out


def solution(mesh):
    specs = (
        P(("dp", "col"), "row"),
        P(("dp", "col"), "row"),
        P("row", "col"),
        P("col", "row"),
    )
    return jax.shard_map(
        shards, mesh=mesh, in_specs=specs, out_specs=specs, check_vma=False
    )
```

time: 1100 us -> 299 us (0.27)
  waiting for transfers between devices: 931 us -> 157 us
  local copies, waits for them, and re-layouts: 41.9 us -> 2.65 us
    psum x1 -> x0, waiting for transfers between devices: 807 us -> none  [shards(): lax.psum(local_in.astype(jnp.bfloat16), 'dp').astype(jnp.float32)]
    ppermute x0 -> x4, waiting for transfers between devices: none -> 51.9 us  [swap(): return lax.ppermute(value, 'dp', [(0, 1), (1, 0)])]
    unnamed x6, local copies, waits for them, and re-layouts: 41.9 us -> 2.65 us
    all_gather x2 -> x4, waiting for transfers between devices: 46.8 us -> 21.9 us  [gather(): return lax.all_gather(value, axis, axis=0, tiled=True)]
  transfers between devices with their start and end apart: 7 -> 12, of which waited for: 7 -> 10; matrix products, arithmetic and copies ran while one was open for 6% -> 22% of each run, Pallas kernels for 0% -> 0%
where the time goes in v1:
time: 299 us
  waiting for transfers between devices  157 us (53%)
  matrix products  76.3 us (26%)
  blocking collectives  39.2 us (13%)
  between operations  14.2 us (5%)
  starting transfers between devices  5.67 us (2%)
  other arithmetic  3.73 us (1%)
    reduce_scatter x4, waiting for transfers between devices, scatter(): return lax.psum_scatter(value, axis, scatter_dimension=0, tiled=True)  83 us
    ppermute x4, waiting for transfers between devices, swap(): return lax.ppermute(value, 'dp', [(0, 1), (1, 0)])  51.9 us
    all_gather x2, blocking collectives, gather(): return lax.all_gather(value, axis, axis=0, tiled=True)  39.2 us
    dot_general x2, matrix products, contract_rows(): lax.dot_general(left, right, (((0,), (0,)), ((), ())), preferred_element_...  32 us
    all_gather x4, waiting for transfers between devices, gather(): return lax.all_gather(value, axis, axis=0, tiled=True)  21.9 us
    dot_general x2, matrix products, contract_cols(): lax.dot_general(left, right, (((1,), (1,)), ((), ())), preferred_element_...  20.8 us
    dot_general x1, matrix products, shards(): pre_part = jnp.dot(group_x, w_in, preferred_element_type=jnp.float32)  12.8 us
    dot_general x1, matrix products, shards(): out_part = jnp.dot(hidden, w_out, preferred_element_type=jnp.float32)  10.7 us
  transfers between devices with their start and end apart: 12, of which 10 were waited for; matrix products, arithmetic and copies ran while one was open for 22% of the time, Pallas kernels for 0%

profile of v1, /device:TPU:0, one launch (start us, length us, event | category | flops | bytes accessed | tf_op | source)
XLA Modules:
  0.0 299.1 jit_solution(1668593751513889281)
XLA Ops:
  7.2 0.0 reduce-scatter.9.cloned.1.call-start
  7.2 21.5 %all_gather.20 = bf16[256,1536]{1,0:T(8,128)(2,1)S(1)} all-gather(bf16[64,1536]{1,0:T(8,128)(2,1)} %param.5), channel_id=1, replica_groups=mesh['dp'=2,'row'=4,'col'=4] {'col'}, dimensions={0}, use_global_device_ids=true | all-gather | bytes 983040 | tf_op jit(solution)/shard_map/all_gather | solution.py:29
  28.7 10.1 %convolution_convert_fusion.2 = bf16[256,6144]{1,0:T(8,128)(2,1)} fusion(bf16[256,1536]{1,0:T(8,128)(2,1)S(1)} %all_gather.20, bf16[6144,1536]{1,0:T(8,128)(2,1)} %param.7), kind=kOutput, calls=%fused_computation.2 | convolution fusion | flops 4833411072 | bytes 22806528 | tf_op jit(solution)/shard_map/dot_general | solution.py:23
  38.9 0.0 reduce-scatter.5.cloned.1.call-start
  38.9 0.9 copy-done.2
  39.8 17.7 %all_gather.18 = bf16[256,1536]{1,0:T(8,128)(2,1)S(1)} all-gather(bf16[64,1536]{1,0:T(8,128)(2,1)S(1)} %copy-done.2), channel_id=1, replica_groups=mesh['dp'=2,'row'=4,'col'=4] {'col'}, dimensions={0}, use_global_device_ids=true | all-gather | bytes 983040 | tf_op jit(solution)/shard_map/all_gather | solution.py:29
  57.5 12.8 %convolution_convert_fusion.3 = bf16[256,6144]{1,0:T(8,128)(2,1)} fusion(bf16[256,1536]{1,0:T(8,128)(2,1)S(1)} %all_gather.18, bf16[1536,6144]{1,0:T(8,128)(2,1)} %param.6), kind=kOutput, calls=%fused_computation.3 | convolution fusion | flops 4833411072 | bytes 22806528 | tf_op jit(solution)/shard_map/dot_general | solution.py:43
  70.3 0.0 all-gather.5.cloned.1.call-start
  70.3 6.0 %reduce-scatter.9.cloned.1.call-done = bf16[64,6144]{1,0:T(8,128)(2,1)} async-done(((bf16[256,6144]{1,0:T(8,128)(2,1)}), bf16[64,6144]{1,0:T(8,128)(2,1)}) %reduce-scatter.9.cloned.1.call-update) | async-done | bytes 786448 | tf_op jit(solution)/shard_map/reduce_scatter | solution.py:37
  76.4 41.3 %reduce-scatter.5.cloned.1.call-done = bf16[64,6144]{1,0:T(8,128)(2,1)} async-done(((bf16[256,6144]{1,0:T(8,128)(2,1)}), bf16[64,6144]{1,0:T(8,128)(2,1)}) %reduce-scatter.5.cloned.1.call-update) | async-done | bytes 786448 | tf_op jit(solution)/shard_map/reduce_scatter | solution.py:37
  117.6 3.7 %fusion.9 = (bf16[64,6144]{1,0:T(8,128)(2,1)}, bf16[64,6144]{1,0:T(8,128)(2,1)}) fusion(bf16[64,6144]{1,0:T(8,128)(2,1)} %reduce-scatter.9.cloned.1.call-done, bf16[64,6144]{1,0:T(8,128)(2,1)} %reduce-scatter.5.cloned.1.call-done), kind=kLoop, calls=%fused_computation.21 | loop fusion | flops 9437184 | bytes 3145728 | tf_op jit(solution)/shard_map/convert_element_type | solution.py:13
  121.4 0.0 all-gather.7.cloned.1.call-start
  121.4 0.5 all-gather.7.cloned.1.call-update
  122.0 1.5 collective-permute-start.1
  123.5 18.0 %collective-permute-done.1 = bf16[64,6144]{1,0:T(8,128)(2,1)S(1)} collective-permute-done((bf16[64,6144]{1,0:T(8,128)(2,1)}, bf16[64,6144]{1,0:T(8,128)(2,1)S(1)}, u32[]{:S(2)}, u32[]{:S(2)}) %collective-permute-start.1) | collective-permute-done | bytes 786464 | tf_op jit(solution)/shard_map/ppermute | solution.py:33
  141.5 0.9 copy-done
  142.5 1.6 collective-permute-start.2
  144.1 17.2 %collective-permute-done.2 = bf16[64,6144]{1,0:T(8,128)(2,1)S(1)} collective-permute-done((bf16[64,6144]{1,0:T(8,128)(2,1)}, bf16[64,6144]{1,0:T(8,128)(2,1)S(1)}, u32[]{:S(2)}, u32[]{:S(2)}) %collective-permute-start.2) | collective-permute-done | bytes 786464 | tf_op jit(solution)/shard_map/ppermute | solution.py:33
  161.3 0.9 copy-done.1
  162.3 10.7 %convolution_convert_fusion.5 = bf16[256,1536]{1,0:T(8,128)(2,1)} fusion(bf16[256,6144]{1,0:T(8,128)(2,1)} %all-gather.5.cloned.1.call-done, bf16[6144,1536]{1,0:T(8,128)(2,1)} %param.7), kind=kOutput, calls=%fused_computation.16 | convolution fusion | flops 4832231424 | bytes 22806528 | tf_op jit(solution)/shard_map/dot_general | solution.py:52
  173.0 0.2 reduce-scatter.11.cloned.1.call-start
  173.3 1.6 collective-permute-start.3
  174.8 0.5 collective-permute-start
  175.4 5.2 %all-gather.7.cloned.1.call-done = bf16[256,6144]{1,0:T(8,128)(2,1)} async-done(((bf16[64,6144]{1,0:T(8,128)(2,1)}), bf16[256,6144]{1,0:T(8,128)(2,1)}) %all-gather.7.cloned.1.call-update) | async-done | bytes 3145744 | tf_op jit(solution)/shard_map/all_gather | solution.py:29
  180.6 10.7 %convolution_convert_fusion.4 = bf16[256,1536]{1,0:T(8,128)(2,1)} fusion(bf16[256,6144]{1,0:T(8,128)(2,1)} %all-gather.7.cloned.1.call-done, bf16[1536,6144]{1,0:T(8,128)(2,1)} %param.6), kind=kOutput, calls=%fused_computation.15 | convolution fusion | flops 4832231424 | bytes 22806528 | tf_op jit(solution)/shard_map/dot_general | solution.py:23
  191.3 16.6 %collective-permute-done = bf16[256,1536]{1,0:T(8,128)(2,1)S(1)} collective-permute-done((bf16[256,1536]{1,0:T(8,128)(2,1)S(1)}, bf16[256,1536]{1,0:T(8,128)(2,1)S(1)}, u32[]{:S(2)}, u32[]{:S(2)}) %collective-permute-start) | collective-permute-done | bytes 786464 | tf_op jit(solution)/shard_map/ppermute | solution.py:33
  207.9 2.6 all-gather.9.cloned.1.call-done
  210.6 16.0 %convolution_convert_fusion = bf16[1536,6144]{1,0:T(8,128)(2,1)} fusion(bf16[256,6144]{1,0:T(8,128)(2,1)} %all-gather.9.cloned.1.call-done, bf16[256,6144]{1,0:T(8,128)(2,1)} %all-gather.7.cloned.1.call-done, bf16[256,1536]{1,0:T(8,128)(2,1)S(1)} %collective-permute-done, bf16[256,1536]{1,0:T(8,128)(2,1)S(1)} %all_gather.18), kind=kOutput, calls=%fused_computation | convolution fusion | flops 9688842240 | bytes 26738688 | tf_op jit(solution)/shard_map/dot_general | solution.py:17
  226.6 14.0 %all-gather.11.cloned.1.call-done = bf16[256,6144]{1,0:T(8,128)(2,1)} async-done(((bf16[64,6144]{1,0:T(8,128)(2,1)}), bf16[256,6144]{1,0:T(8,128)(2,1)}) %all-gather.11.cloned.1.call-update) | async-done | bytes 3145744 | tf_op jit(solution)/shard_map/all_gather | solution.py:29
  240.6 16.0 %convolution_convert_fusion.1 = bf16[6144,1536]{1,0:T(8,128)(2,1)} fusion(bf16[256,6144]{1,0:T(8,128)(2,1)} %all-gather.11.cloned.1.call-done, bf16[256,6144]{1,0:T(8,128)(2,1)} %all-gather.5.cloned.1.call-done, bf16[256,1536]{1,0:T(8,128)(2,1)S(1)} %collective-permute-done.3, bf16[256,1536]{1,0:T(8,128)(2,1)S(1)} %all_gather.20), kind=kOutput, calls=%fused_computation.1 | convolution fusion | flops 9688842240 | bytes 26738688 | tf_op jit(solution)/shard_map/dot_general | solution.py:17
  256.6 10.2 %reduce-scatter.7.cloned.1.call-done = bf16[64,1536]{1,0:T(8,128)(2,1)} async-done(((bf16[256,1536]{1,0:T(8,128)(2,1)}), bf16[64,1536]{1,0:T(8,128)(2,1)}) %reduce-scatter.7.cloned.1.call-update) | async-done | bytes 196624 | tf_op jit(solution)/shard_map/reduce_scatter | solution.py:37
  266.8 25.5 %reduce-scatter.11.cloned.1.call-done = bf16[64,1536]{1,0:T(8,128)(2,1)} async-done(((bf16[256,1536]{1,0:T(8,128)(2,1)}), bf16[64,1536]{1,0:T(8,128)(2,1)}) %reduce-scatter.11.cloned.1.call-update) | async-done | bytes 196624 | tf_op jit(solution)/shard_map/reduce_scatter | solution.py:37
  (15 shorter events, 0.3 us)
Async XLA Ops:
  7.2 69.2 %reduce-scatter.9.cloned.1.call-start = ((), (), s32[]{:S(2)}) async-start(), calls=%async_computation.7 | async-start | bytes 3932160 | tf_op jit(solution)/shard_map/reduce_scatter | solution.py:37
  38.9 0.9 copy-start.2
  38.9 78.7 %reduce-scatter.5.cloned.1.call-start = ((), (), s32[]{:S(2)}) async-start(), calls=%async_computation.4 | async-start | bytes 3932160 | tf_op jit(solution)/shard_map/reduce_scatter | solution.py:37
  70.3 92.0 %all-gather.5.cloned.1.call-start = ((), (), s32[]{:S(2)}) async-start(), calls=%async_computation.5 | async-start | bytes 3932160 | tf_op jit(solution)/shard_map/all_gather | solution.py:29
  121.4 59.2 %all-gather.7.cloned.1.call-start = ((), (), s32[]{:S(2)}) async-start(), calls=%async_computation.8 | async-start | bytes 3932160 | tf_op jit(solution)/shard_map/all_gather | solution.py:29
  121.9 88.6 %all-gather.9.cloned.1.call-start = ((), (), s32[]{:S(2)}) async-start(), calls=%async_computation.10 | async-start | bytes 3932160 | tf_op jit(solution)/shard_map/all_gather | solution.py:29
  122.0 19.5 %collective-permute-start.1 = (bf16[64,6144]{1,0:T(8,128)(2,1)}, bf16[64,6144]{1,0:T(8,128)(2,1)S(1)}, u32[]{:S(2)}, u32[]{:S(2)}) collective-permute-start(bf16[64,6144]{1,0:T(8,128)(2,1)} %get-tuple-element.4), channel_id=1, source_target_pairs={{0,16},{16,0},{1,17},{17,1},{2,18},{18,2},{3,19},{19,3},{4,20},{20... | collective-permute-start | bytes 2359304 | tf_op jit(solution)/shard_map/ppermute | solution.py:33
  141.5 0.9 copy-start
  142.5 98.1 %all-gather.11.cloned.1.call-start = ((), (), s32[]{:S(2)}) async-start(), calls=%async_computation.11 | async-start | bytes 3932160 | tf_op jit(solution)/shard_map/all_gather | solution.py:29
  142.5 18.8 %collective-permute-start.2 = (bf16[64,6144]{1,0:T(8,128)(2,1)}, bf16[64,6144]{1,0:T(8,128)(2,1)S(1)}, u32[]{:S(2)}, u32[]{:S(2)}) collective-permute-start(bf16[64,6144]{1,0:T(8,128)(2,1)} %get-tuple-element.5), channel_id=1, source_target_pairs={{0,16},{16,0},{1,17},{17,1},{2,18},{18,2},{3,19},{19,3},{4,20},{20... | collective-permute-start | bytes 2359304 | tf_op jit(solution)/shard_map/ppermute | solution.py:33
  161.3 0.9 copy-start.1
  162.2 104.6 %reduce-scatter.7.cloned.1.call-start = ((), (), s32[]{:S(2)}) async-start(), calls=%async_computation.6 | async-start | bytes 983040 | tf_op jit(solution)/shard_map/reduce_scatter | solution.py:37
  173.0 119.2 %reduce-scatter.11.cloned.1.call-start = ((), (), s32[]{:S(2)}) async-start(), calls=%async_computation.9 | async-start | bytes 983040 | tf_op jit(solution)/shard_map/reduce_scatter | solution.py:37
  173.3 53.3 %collective-permute-start.3 = (bf16[256,1536]{1,0:T(8,128)(2,1)S(1)}, bf16[256,1536]{1,0:T(8,128)(2,1)S(1)}, u32[]{:S(2)}, u32[]{:S(2)}) collective-permute-start(bf16[256,1536]{1,0:T(8,128)(2,1)S(1)} %all_gather.20), channel_id=1, source_target_pairs={{0,16},{16,0},{1,17},{17,1},{2,18},{18,2},{3,19},{19,3},{4,20},{20... | collective-permute-start | bytes 2359304 | tf_op jit(solution)/shard_map/ppermute | solution.py:33
  174.8 33.1 %collective-permute-start = (bf16[256,1536]{1,0:T(8,128)(2,1)S(1)}, bf16[256,1536]{1,0:T(8,128)(2,1)S(1)}, u32[]{:S(2)}, u32[]{:S(2)}) collective-permute-start(bf16[256,1536]{1,0:T(8,128)(2,1)S(1)} %all_gather.18), channel_id=1, source_target_pairs={{0,16},{16,0},{1,17},{17,1},{2,18},{18,2},{3,19},{19,3},{4,20},{20... | collective-permute-start | bytes 2359304 | tf_op jit(solution)/shard_map/ppermute | solution.py:33
Sparse Core Ops, SparseCore 0:
  39.0 37.3 reduce-scatter.8
  79.6 37.9 reduce-scatter.4
  121.5 28.5 all-gather.4
  152.0 28.5 all-gather.6
  182.0 28.5 all-gather.8
  212.0 28.5 all-gather.10
  243.4 23.2 reduce-scatter.6
  269.6 22.5 reduce-scatter.10

commit v2 on v1

v2 whole, which is shorter than its diff:
```python
import functools
import math

import jax
import jax.numpy as jnp
from jax import lax
from jax.experimental import pallas as pl
from jax.experimental.pallas import tpu as pltpu
from jax.sharding import PartitionSpec as P

MESH = pl.DeviceIdType.MESH
F32 = jnp.float32
BF16 = jnp.bfloat16
SCALE = math.sqrt(2.0 / math.pi)
CUBIC = 0.044715


def contract_rows(left, right):
    return lax.dot_general(
        left, right, (((0,), (0,)), ((), ())), preferred_element_type=F32
    )


def contract_cols(left, right):
    return lax.dot_general(
        left, right, (((1,), (1,)), ((), ())), preferred_element_type=F32
    )


def tile_of(size, largest):
    tile = largest
    while size % tile:
        tile -= 128
    return tile


def middle(
    sizes,
    x_ref, dy_ref, w_in, w_out,
    out_ref, back_ref, hid_all, gp_all, x_all, dy_all,
    xg, parts, crecv, ysend, yrecv, gat, wa_in, wa_out, we_in, we_out,
    acc_out, acc_back,
    x_local, x_ssem, x_rsem, d_ssem, d_rsem,
    c_ssem, c_rsem, y_ssem, y_rsem, ag_rsem, ag_y, ag_x, ag_c,
    wa_sem, we_sem, o_sem, xo_sem,
):
    n_col, n_y, chunks, width = sizes
    rows, depth = x_ref.shape
    group = rows * n_col
    share = group // (2 * n_y)
    me_dp, me_row, me_col = (lax.axis_index(a) for a in ("dp", "row", "col"))
    me_y, me_k = me_row // 2, me_row % 2
    other_dp, other_k = 1 - me_dp, 1 - me_k

    def y_peer(d):
        return lax.rem(me_y + d, n_y)

    def y_from(d):
        return lax.rem(me_y + n_y - d, n_y)

    def col_peer(d):
        return lax.rem(me_col + d, n_col)

    def col_from(d):
        return lax.rem(me_col + n_col - d, n_col)

    def remote(src, dst, ssem, rsem, peer):
        return pltpu.make_async_remote_copy(
            src_ref=src, dst_ref=dst, send_sem=ssem, recv_sem=rsem,
            device_id=peer, device_id_type=MESH,
        )

    to_core = {"row": me_y * 2 + other_k}
    to_dp = {"dp": other_dp}

    barrier = pltpu.get_barrier_semaphore()
    peers = [to_core, to_dp]
    peers += [{"row": y_peer(d) * 2 + me_k} for d in range(1, n_y)]
    peers += [{"col": col_peer(d)} for d in range(1, n_col)]
    for peer in peers:
        pl.semaphore_signal(barrier, inc=1, device_id=peer, device_id_type=MESH)

    def load_a(c, slot):
        cols = pl.ds(pl.multiple_of(c * width, width), width)
        return (
            pltpu.make_async_copy(w_in.at[:, cols], wa_in.at[slot], wa_sem.at[slot, 0]),
            pltpu.make_async_copy(w_out.at[cols, :], wa_out.at[slot], wa_sem.at[slot, 1]),
        )

    def load_e(c, slot):
        cols = pl.ds(pl.multiple_of(c * width, width), width)
        return (
            pltpu.make_async_copy(w_in.at[:, cols], we_in.at[slot], we_sem.at[slot, 0]),
            pltpu.make_async_copy(w_out.at[cols, :], we_out.at[slot], we_sem.at[slot, 1]),
        )

    for copy in load_a(0, 0):
        copy.start()
    own = [
        pltpu.make_async_copy(ref, xg.at[a, me_dp, me_col], x_local.at[a])
        for a, ref in enumerate((x_ref, dy_ref))
    ]
    for copy in own:
        copy.start()
    acc_out[...] = jnp.zeros_like(acc_out)
    acc_back[...] = jnp.zeros_like(acc_back)
    pl.semaphore_wait(barrier, len(peers))

    def x_copy(a, d, at):
        ref = (x_ref, dy_ref)[a]
        return remote(
            ref, xg.at[a, me_dp, at], x_ssem.at[a, d - 1], x_rsem.at[a, d - 1],
            {"col": col_peer(d)},
        )

    for a in range(2):
        for d in range(1, n_col):
            x_copy(a, d, me_col).start()
    for copy in own:
        copy.wait()
    for a in range(2):
        for d in range(1, n_col):
            x_copy(a, d, col_from(d)).wait_recv()

    def d_copy(a, dp):
        return remote(xg.at[a, dp], xg.at[a, dp], d_ssem.at[a], d_rsem.at[a], to_dp)

    for a in range(2):
        d_copy(a, me_dp).start()

    def core_copy(c, k):
        return remote(parts.at[c, k], crecv.at[c], c_ssem.at[c], c_rsem.at[c], to_core)

    def y_copy(c, d):
        return remote(
            ysend.at[c, d - 1], yrecv.at[c, d - 1], y_ssem.at[c, d - 1],
            y_rsem.at[c, d - 1], {"row": y_peer(d) * 2 + me_k},
        )

    def piece(c, dp, y, k):
        return gat.at[c, :, dp, y, k]

    def share_copy(c, dp, y, k, ssem, peer):
        ref = piece(c, dp, y, k)
        return remote(ref, ref, ssem, ag_rsem.at[c, dp, y, k], peer)

    def ag_y_copy(c, d, y):
        return share_copy(c, me_dp, y, me_k, ag_y.at[c, d - 1], {"row": y_peer(d) * 2 + me_k})

    def ag_x_copy(c, dp, y):
        return share_copy(c, dp, y, me_k, ag_x.at[c, y], to_dp)

    def ag_c_copy(c, dp, y, k):
        return share_copy(c, dp, y, k, ag_c.at[c, dp, y], to_core)

    def out_copy(c, a):
        cols = pl.ds(pl.multiple_of(c * width, width), width)
        return pltpu.make_async_copy(
            gat.at[c, a], (hid_all, gp_all)[a].at[:, :, :, :, cols], o_sem.at[c, a]
        )

    n_tile = tile_of(width, 256)
    d_tile = tile_of(depth, 256)

    def stage_a(c):
        slot = lax.rem(c, 2)

        @pl.when(c + 1 < chunks)
        def _():
            for copy in load_a(c + 1, 1 - slot):
                copy.start()

        for copy in load_a(c, slot):
            copy.wait()
        x = xg[0, me_dp].reshape(group, depth)
        dy = xg[1, me_dp].reshape(group, depth)
        for t in range(width // n_tile):
            cols = slice(t * n_tile, (t + 1) * n_tile)
            pre = jnp.dot(x, wa_in[slot, :, cols], preferred_element_type=F32)
            grad = contract_cols(dy, wa_out[slot, cols, :])
            for a, part in enumerate((pre, grad)):
                part = part.astype(BF16)
                for r in range(2 * n_y):
                    parts[c, r % 2, a, r // 2, :, cols] = part[r * share:(r + 1) * share]
        core_copy(c, other_k).start()

    def stage_b(c):
        core_copy(c, me_k).wait_recv()
        for d in range(1, n_y):
            y = y_peer(d)
            for a in range(2):
                ysend[c, d - 1, a] = (
                    parts[c, me_k, a, y].astype(F32) + crecv[c, a, y].astype(F32)
                ).astype(BF16)
            y_copy(c, d).start()

    def stage_c(c):
        for d in range(1, n_y):
            y_copy(c, d).wait_recv()
        for t in range(width // n_tile):
            cols = slice(t * n_tile, (t + 1) * n_tile)

            def total(a):
                value = parts[c, me_k, a, me_y, :, cols].astype(F32)
                value = value + crecv[c, a, me_y, :, cols].astype(F32)
                for d in range(1, n_y):
                    value = value + yrecv[c, d - 1, a, :, cols].astype(F32)
                return value

            pre, grad = total(0), total(1)
            square = pre * pre
            bend = jnp.tanh(SCALE * (pre + CUBIC * (square * pre)))
            half = 0.5 * (1.0 + bend)
            slope = half + (0.5 * pre) * (1.0 - bend * bend) * (
                SCALE * (1.0 + (3.0 * CUBIC) * square)
            )
            gat[c, 0, me_dp, me_y, me_k, :, cols] = (pre * half).astype(BF16)
            gat[c, 1, me_dp, me_y, me_k, :, cols] = (grad * slope).astype(BF16)
        for d in range(1, n_y):
            ag_y_copy(c, d, me_y).start()
        ag_x_copy(c, me_dp, me_y).start()
        ag_c_copy(c, me_dp, me_y, me_k).start()

    def stage_d(c):
        for d in range(1, n_y):
            y = y_from(d)
            ag_y_copy(c, d, y).wait_recv()
            ag_c_copy(c, me_dp, y, me_k).start()
            ag_x_copy(c, me_dp, y).start()

    def stage_e(c):
        slot = lax.rem(c, 2)

        @pl.when(c + 1 < chunks)
        def _():
            for copy in load_e(c + 1, 1 - slot):
                copy.start()

        for y in range(n_y):
            ag_c_copy(c, me_dp, y, other_k).wait_recv()
        for copy in load_e(c, slot):
            copy.wait()
        hidden = gat[c, 0, me_dp].reshape(group, width)
        grad_pre = gat[c, 1, me_dp].reshape(group, width)
        for t in range(depth // d_tile):
            cols = slice(t * d_tile, (t + 1) * d_tile)
            acc_out[:, cols] += jnp.dot(
                hidden, we_out[slot, :, cols], preferred_element_type=F32
            )
            acc_back[:, cols] += contract_cols(grad_pre, we_in[slot, cols, :])
        for y in range(n_y):
            ag_x_copy(c, other_dp, y).wait_recv()
            ag_c_copy(c, other_dp, y, me_k).start()

    def stage_f(c):
        for y in range(n_y):
            ag_c_copy(c, other_dp, y, other_k).wait_recv()
        for a in range(2):
            out_copy(c, a).start()

    def step(i, carry):
        @pl.when(i == 1)
        def _():
            for copy in load_e(0, 0):
                copy.start()

        for lag, stage in enumerate((stage_a, stage_b, stage_c, stage_d, stage_e, stage_f)):
            @pl.when(jnp.logical_and(i >= lag, i < chunks + lag))
            def _(lag=lag, stage=stage):
                stage(i - lag)

        return carry

    lax.fori_loop(0, chunks + 5, step, 0)

    out_ref[...] = acc_out[...].astype(BF16)
    back_ref[...] = acc_back[...].astype(BF16)
    x_out = []
    for a in range(2):
        d_copy(a, other_dp).wait_recv()
        x_out.append(pltpu.make_async_copy(xg.at[a], (x_all, dy_all)[a], xo_sem.at[a]))
        x_out[a].start()
    for a in range(2):
        d_copy(a, me_dp).wait_send()
        for d in range(1, n_col):
            x_copy(a, d, me_col).wait_send()

    def drain(c, carry):
        core_copy(c, other_k).wait_send()
        for d in range(1, n_y):
            y_copy(c, d).wait_send()
            ag_y_copy(c, d, me_y).wait_send()
        for y in range(n_y):
            ag_x_copy(c, me_dp, y).wait_send()
            for dp in range(2):
                ag_c_copy(c, dp, y, me_k).wait_send()
        for a in range(2):
            out_copy(c, a).wait()
        return carry

    lax.fori_loop(0, chunks, drain, 0)
    for copy in x_out:
        copy.wait()


def shards(mesh, tokens, grad_out, w_in, w_out):
    n_col, n_y = mesh.shape["col"], mesh.shape["row"] // 2
    rows, depth = tokens.shape
    hidden_units = w_in.shape[1]
    group = rows * n_col
    share = group // (2 * n_y)
    width = tile_of(hidden_units, 768)
    chunks = hidden_units // width
    dma = pltpu.SemaphoreType.DMA
    vmem, any_space = pl.BlockSpec(memory_space=pltpu.VMEM), pl.BlockSpec(memory_space=pl.ANY)
    shape = jax.ShapeDtypeStruct
    out_part, back_part, hid, gp, x_all, dy_all = pl.pallas_call(
        functools.partial(middle, (n_col, n_y, chunks, width)),
        out_shape=(
            shape((group, depth), BF16),
            shape((group, depth), BF16),
            shape((2, n_y, 2, share, hidden_units), BF16),
            shape((2, n_y, 2, share, hidden_units), BF16),
            shape((2, n_col, rows, depth), BF16),
            shape((2, n_col, rows, depth), BF16),
        ),
        in_specs=[vmem, vmem, any_space, any_space],
        out_specs=[vmem, vmem] + [any_space] * 4,
        scratch_shapes=[
            pltpu.VMEM((2, 2, n_col, rows, depth), BF16),
            pltpu.VMEM((chunks, 2, 2, n_y, share, width), BF16),
            pltpu.VMEM((chunks, 2, n_y, share, width), BF16),
            pltpu.VMEM((chunks, n_y - 1, 2, share, width), BF16),
            pltpu.VMEM((chunks, n_y - 1, 2, share, width), BF16),
            pltpu.VMEM((chunks, 2, 2, n_y, 2, share, width), BF16),
            pltpu.VMEM((2, depth, width), BF16),
            pltpu.VMEM((2, width, depth), BF16),
            pltpu.VMEM((2, depth, width), BF16),
            pltpu.VMEM((2, width, depth), BF16),
            pltpu.VMEM((group, depth), F32),
            pltpu.VMEM((group, depth), F32),
            dma((2,)),
            dma((2, n_col - 1)),
            dma((2, n_col - 1)),
            dma((2,)),
            dma((2,)),
            dma((chunks,)),
            dma((chunks,)),
            dma((chunks, n_y - 1)),
            dma((chunks, n_y - 1)),
            dma((chunks, 2, n_y, 2)),
            dma((chunks, n_y - 1)),
            dma((chunks, n_y)),
            dma((chunks, 2, n_y)),
            dma((2, 2)),
            dma((2, 2)),
            dma((chunks, 2)),
            dma((2,)),
        ],
        compiler_params=pltpu.CompilerParams(
            collective_id=0, has_side_effects=True, vmem_limit_bytes=60 * 2**20
        ),
        cost_estimate=pl.CostEstimate(
            flops=8 * group * depth * hidden_units,
            bytes_accessed=8 * depth * hidden_units,
            transcendentals=0,
        ),
        name="middle",
    )(tokens, grad_out, w_in, w_out)
    output = lax.psum_scatter(out_part, "col", scatter_dimension=0, tiled=True)
    grad_tokens = lax.psum_scatter(back_part, "col", scatter_dimension=0, tiled=True)
    both = 2 * group
    grad_w_out = contract_rows(
        hid.reshape(both, hidden_units), dy_all.reshape(both, depth)
    ).astype(BF16)
    grad_w_in = contract_rows(
        x_all.reshape(both, depth), gp.reshape(both, hidden_units)
    ).astype(BF16)
    return output, grad_tokens, grad_w_in, grad_w_out


def solution(mesh):
    specs = (
        P(("dp", "col"), "row"),
        P(("dp", "col"), "row"),
        P("row", "col"),
        P("col", "row"),
    )
    return jax.shard_map(
        functools.partial(shards, mesh),
        mesh=mesh, in_specs=specs, out_specs=specs, check_vma=False,
    )
```

time: 299 us -> 212 us (0.71)
  Pallas kernels: 0 us -> 145 us
  waiting for transfers between devices: 157 us -> 22.9 us
  matrix products: 76.3 us -> 29.7 us
  blocking collectives: 39.2 us -> 0 us
  starting transfers between devices: 5.67 us -> 0.26 us
  other arithmetic: 3.73 us -> 0.01 us
    pallas_call x0 -> x1, Pallas kernels: none -> 145 us  [shards(): pl.pallas_call(functools.partial(middle, (n_col, n_y, chunks, width)), ou...]
    reduce_scatter x4 -> x2, waiting for transfers between devices: 83 us -> 22.4 us  [the longest x1 22.4 us: shards(): lax.psum_scatter(back_part, 'col', scatter_dimension=0, tiled=True)]
    ppermute x4 -> x0, waiting for transfers between devices: 51.9 us -> none  [swap(): return lax.ppermute(value, 'dp', [(0, 1), (1, 0)])]
    dot_general x4 -> x0, matrix products: 44.3 us -> none  [the longest x2 20.8 us: contract_cols(): lax.dot_general(left, right, (((1,), (1,)), ((), ())), preferred_element_...]
    all_gather x2 -> x0, blocking collectives: 39.2 us -> none  [gather(): return lax.all_gather(value, axis, axis=0, tiled=True)]
    all_gather x4 -> x0, waiting for transfers between devices: 21.9 us -> none  [gather(): return lax.all_gather(value, axis, axis=0, tiled=True)]
    ppermute x4 -> x0, starting transfers between devices: 5.17 us -> none  [swap(): return lax.ppermute(value, 'dp', [(0, 1), (1, 0)])]
    convert_element_type x1 -> x0, other arithmetic: 3.73 us -> none  [gelu_back(): return pullback(grad_hidden)[0].astype(jnp.bfloat16)]
  transfers between devices with their start and end apart: 12 -> 2, of which waited for: 10 -> 1; matrix products, arithmetic and copies ran while one was open for 22% -> 14% of each run, Pallas kernels for 0% -> 0%
where the time goes in v2:
time: 212 us
  Pallas kernels  145 us (68%)
  matrix products  29.7 us (14%)
  waiting for transfers between devices  22.9 us (11%)
  between operations  14.1 us (7%)
    pallas_call x1, Pallas kernels, shards(): pl.pallas_call(functools.partial(middle, (n_col, n_y, chunks, width)), ou...  145 us
    dot_general x2, matrix products, contract_rows(): lax.dot_general(left, right, (((0,), (0,)), ((), ())), preferred_element_...  29.7 us
    reduce_scatter x1, waiting for transfers between devices, shards(): lax.psum_scatter(back_part, 'col', scatter_dimension=0, tiled=True)  22.4 us
  transfers between devices with their start and end apart: 2, of which 1 were waited for; matrix products, arithmetic and copies ran while one was open for 14% of the time, Pallas kernels for 0%

profile of v2, /device:TPU:0, one launch (start us, length us, event | category | flops | bytes accessed | tf_op | source)
XLA Modules:
  0.0 211.7 jit_solution(11768550382292937543)
XLA Ops:
  7.2 0.0 reduce-scatter.3.cloned.1.call-start
  7.2 144.7 %middle.1 = (bf16[256,1536]{1,0:T(8,128)(2,1)}, bf16[256,1536]{1,0:T(8,128)(2,1)}, bf16[2,2,2,64,6144]{4,3,2,1,0:T(8,128)(2,1)}, bf16[2,2,2,64,6144]{4,3,2,1,0:T...) custom-call(bf16[64,1536]{1,0:T(8,128)(2,1)} %x_ref.1, bf16[64,1536]{1,0:T(8,128)(2,1)} %dy_ref.1, ...), custom_call_target="tpu_custom_call" | custom-call | flops 19327352832 | bytes 75497472 | tf_op jit(solution)/shard_map/middle/pallas_call | solution.py:317
  151.9 0.0 reduce-scatter.3.cloned.1.call-update
  152.0 0.2 reduce-scatter.5.cloned.1.call-start
  152.2 0.0 slice-start
  152.2 0.5 reduce-scatter.5.cloned.1.call-update
  152.7 0.0 slice-start.1
  152.7 0.0 copy-start
  152.7 16.5 %convolution_convert_fusion.1 = bf16[6144,1536]{1,0:T(8,128)(2,1)} fusion(bf16[512,6144]{1,0:T(8,128)(2,1)} %bitcast.11, bf16[512,1536]{1,0:T(8,128)(2,1)} %bitcast.13), kind=kOutput, calls=%fused_computation.1 | convolution fusion | flops 9673113600 | bytes 26738688 | tf_op jit(solution)/shard_map/dot_general | solution.py:19
  169.2 0.0 slice-done
  169.2 0.0 slice-done.1
  169.2 0.0 copy-done
  169.2 13.2 %convolution_convert_fusion = bf16[1536,6144]{1,0:T(8,128)(2,1)} fusion(bf16[512,1536]{1,0:T(8,128)(2,1)S(1)} %bitcast.12, bf16[512,6144]{1,0:T(8,128)(2,1)S(1)} %bitcast.10), kind=kOutput, calls=%fused_computation | convolution fusion | flops 9673113600 | bytes 26738688 | tf_op jit(solution)/shard_map/dot_general | solution.py:19
  182.4 0.0 reduce-scatter.3.cloned.1.call-done
  182.4 22.4 %reduce-scatter.5.cloned.1.call-done = bf16[64,1536]{1,0:T(8,128)(2,1)} async-done(((bf16[256,1536]{1,0:T(8,128)(2,1)}), bf16[64,1536]{1,0:T(8,128)(2,1)}) %reduce-scatter.5.cloned.1.call-update) | async-done | bytes 196624 | tf_op jit(solution)/shard_map/reduce_scatter | solution.py:371
  (1 shorter events, 0.0 us)
Async XLA Ops:
  7.2 175.3 %reduce-scatter.3.cloned.1.call-start = ((), (), s32[]{:S(2)}) async-start(), calls=%async_computation.2 | async-start | bytes 983040 | tf_op jit(solution)/shard_map/reduce_scatter | solution.py:370
  152.0 52.9 %reduce-scatter.5.cloned.1.call-start = ((), (), s32[]{:S(2)}) async-start(), calls=%async_computation.3 | async-start | bytes 983040 | tf_op jit(solution)/shard_map/reduce_scatter | solution.py:371
  152.2 17.0 %slice-start = ((s8[6291456]{0:T(1024)(128)(4,1)}), s8[2097152]{0:T(1024)(128)(4,1)S(1)}, s32[]{:S(2)}) async-start(s8[6291456]{0:T(1024)(128)(4,1)} %bitcast.8), calls=%async_computation.4 | async-start | bytes 4194304
  152.7 16.5 %slice-start.1 = ((s8[6291456]{0:T(1024)(128)(4,1)}), s8[4194304]{0:T(1024)(128)(4,1)S(1)}, s32[]{:S(2)}) async-start(s8[6291456]{0:T(1024)(128)(4,1)} %bitcast.8), calls=%async_computation.5 | async-start | bytes 8388608
  152.7 16.5 %copy-start = (bf16[2,4,64,1536]{3,2,1,0:T(8,128)(2,1)S(1)}, bf16[2,4,64,1536]{3,2,1,0:T(8,128)(2,1)}, u32[]{:S(2)}) copy-start(bf16[2,4,64,1536]{3,2,1,0:T(8,128)(2,1)} %get-tuple-element.12) | copy-start | bytes 4718596
Sparse Core Ops, SparseCore 0:
  152.1 27.2 reduce-scatter.2
  182.3 22.5 reduce-scatter.4

commit v3 on v2

--- a/solution.py
+++ b/solution.py
@@ -37,7 +37,7 @@
 def middle(
     sizes,
     x_ref, dy_ref, w_in, w_out,
-    out_ref, back_ref, hid_all, gp_all, x_all, dy_all,
+    out_ref, hid_all, gp_all, x_all, dy_all,
     xg, parts, crecv, ysend, yrecv, gat, wa_in, wa_out, we_in, we_out,
     acc_out, acc_back,
     x_local, x_ssem, x_rsem, d_ssem, d_rsem,
@@ -118,15 +118,17 @@
             x_copy(a, d, me_col).start()
     for copy in own:
         copy.wait()
+
+    def d_copy(a, dp, d):
+        ref = xg.at[a, dp, col_from(d)]
+        return remote(ref, ref, d_ssem.at[a, d], d_rsem.at[a, d], to_dp)
+
+    for a in range(2):
+        d_copy(a, me_dp, 0).start()
     for a in range(2):
         for d in range(1, n_col):
             x_copy(a, d, col_from(d)).wait_recv()
-
-    def d_copy(a, dp):
-        return remote(xg.at[a, dp], xg.at[a, dp], d_ssem.at[a], d_rsem.at[a], to_dp)
-
-    for a in range(2):
-        d_copy(a, me_dp).start()
+            d_copy(a, me_dp, d).start()
 
     def core_copy(c, k):
         return remote(parts.at[c, k], crecv.at[c], c_ssem.at[c], c_rsem.at[c], to_core)
@@ -248,6 +250,8 @@
                 hidden, we_out[slot, :, cols], preferred_element_type=F32
             )
             acc_back[:, cols] += contract_cols(grad_pre, we_in[slot, cols, :])
+
+    def stage_g(c):
         for y in range(n_y):
             ag_x_copy(c, other_dp, y).wait_recv()
             ag_c_copy(c, other_dp, y, me_k).start()
@@ -258,30 +262,38 @@
         for a in range(2):
             out_copy(c, a).start()
 
+    last = 7
+
     def step(i, carry):
         @pl.when(i == 1)
         def _():
             for copy in load_e(0, 0):
                 copy.start()
 
-        for lag, stage in enumerate((stage_a, stage_b, stage_c, stage_d, stage_e, stage_f)):
+        stages = (
+            (0, stage_a), (1, stage_b), (2, stage_c), (3, stage_d), (4, stage_e),
+            (last - 1, stage_g), (last, stage_f),
+        )
+        for lag, stage in stages:
             @pl.when(jnp.logical_and(i >= lag, i < chunks + lag))
             def _(lag=lag, stage=stage):
                 stage(i - lag)
 
         return carry
 
-    lax.fori_loop(0, chunks + 5, step, 0)
-
-    out_ref[...] = acc_out[...].astype(BF16)
-    back_ref[...] = acc_back[...].astype(BF16)
+    lax.fori_loop(0, chunks + last, step, 0)
+
+    out_ref[:, :depth] = acc_out[...].astype(BF16)
+    out_ref[:, depth:] = acc_back[...].astype(BF16)
     x_out = []
     for a in range(2):
-        d_copy(a, other_dp).wait_recv()
+        for d in range(n_col):
+            d_copy(a, other_dp, d).wait_recv()
         x_out.append(pltpu.make_async_copy(xg.at[a], (x_all, dy_all)[a], xo_sem.at[a]))
         x_out[a].start()
     for a in range(2):
-        d_copy(a, me_dp).wait_send()
+        for d in range(n_col):
+            d_copy(a, me_dp, d).wait_send()
         for d in range(1, n_col):
             x_copy(a, d, me_col).wait_send()
 
@@ -314,18 +326,17 @@
     dma = pltpu.SemaphoreType.DMA
     vmem, any_space = pl.BlockSpec(memory_space=pltpu.VMEM), pl.BlockSpec(memory_space=pl.ANY)
     shape = jax.ShapeDtypeStruct
-    out_part, back_part, hid, gp, x_all, dy_all = pl.pallas_call(
+    part, hid, gp, x_all, dy_all = pl.pallas_call(
         functools.partial(middle, (n_col, n_y, chunks, width)),
         out_shape=(
-            shape((group, depth), BF16),
-            shape((group, depth), BF16),
+            shape((group, 2 * depth), BF16),
             shape((2, n_y, 2, share, hidden_units), BF16),
             shape((2, n_y, 2, share, hidden_units), BF16),
             shape((2, n_col, rows, depth), BF16),
             shape((2, n_col, rows, depth), BF16),
         ),
         in_specs=[vmem, vmem, any_space, any_space],
-        out_specs=[vmem, vmem] + [any_space] * 4,
+        out_specs=[vmem] + [any_space] * 4,
         scratch_shapes=[
             pltpu.VMEM((2, 2, n_col, rows, depth), BF16),
             pltpu.VMEM((chunks, 2, 2, n_y, share, width), BF16),
@@ -342,8 +353,8 @@
             dma((2,)),
             dma((2, n_col - 1)),
             dma((2, n_col - 1)),
-            dma((2,)),
-            dma((2,)),
+            dma((2, n_col)),
+            dma((2, n_col)),
             dma((chunks,)),
             dma((chunks,)),
             dma((chunks, n_y - 1)),
@@ -367,8 +378,8 @@
         ),
         name="middle",
     )(tokens, grad_out, w_in, w_out)
-    output = lax.psum_scatter(out_part, "col", scatter_dimension=0, tiled=True)
-    grad_tokens = lax.psum_scatter(back_part, "col", scatter_dimension=0, tiled=True)
+    total = lax.psum_scatter(part, "col", scatter_dimension=0, tiled=True)
+    output, grad_tokens = total[:, :depth], total[:, depth:]
     both = 2 * group
     grad_w_out = contract_rows(
         hid.reshape(both, hidden_units), dy_all.reshape(both, depth)

time: 212 us -> 177 us (0.83)
  Pallas kernels: 145 us -> 123 us
  waiting for transfers between devices: 22.9 us -> 8.21 us
    pallas_call x1, Pallas kernels: 145 us -> 123 us  [shards(): pl.pallas_call(functools.partial(middle, (n_col, n_y, chunks, width)), ou...]
    reduce_scatter x2 -> x1, waiting for transfers between devices: 22.4 us -> 8.19 us  [shards(): total = lax.psum_scatter(part, 'col', scatter_dimension=0, tiled=True)]
  transfers between devices with their start and end apart: 2 -> 1, of which waited for: 1 -> 1; matrix products, arithmetic and copies ran while one was open for 14% -> 17% of each run, Pallas kernels for 0% -> 0%
where the time goes in v3:
time: 177 us; the launch traced here: 176 us
  Pallas kernels  123 us (69%)
  matrix products  29.7 us (17%)
  between operations  14.1 us (8%)
  waiting for transfers between devices  8.21 us (5%)
  local copies, waits for them, and re-layouts  1.8 us (1%)
    pallas_call x1, Pallas kernels, shards(): pl.pallas_call(functools.partial(middle, (n_col, n_y, chunks, width)), ou...  123 us
    dot_general x2, matrix products, contract_rows(): lax.dot_general(left, right, (((0,), (0,)), ((), ())), preferred_element_...  29.7 us
    reduce_scatter x1, waiting for transfers between devices, shards(): total = lax.psum_scatter(part, 'col', scatter_dimension=0, tiled=True)  8.19 us
  transfers between devices with their start and end apart: 1, of which 1 were waited for; matrix products, arithmetic and copies ran while one was open for 17% of the time, Pallas kernels for 0%

profile of v3, /device:TPU:0, one launch (start us, length us, event | category | flops | bytes accessed | tf_op | source)
XLA Modules:
  0.0 176.5 jit_solution(9776042218207778133)
XLA Ops:
  7.2 0.0 reduce-scatter.2.cloned.1.call-start
  7.2 122.6 %middle.1 = (bf16[256,3072]{1,0:T(8,128)(2,1)}, bf16[2,2,2,64,6144]{4,3,2,1,0:T(8,128)(2,1)}, bf16[2,2,2,64,6144]{4,3,2,1,0:T(8,128)(2,1)}, bf16[2,4,64,1536]{3,2,1,0:T(8,128)(2,1)}, bf16[2,4,64,1536]{3,2,1,0:T(8,128)(2,1)}) custom-call(bf16[64,1536]{1,0:T(8,128)(2,1)} %x_ref.1, bf16[64,1536]{1,0:T(8,128)(2,1)} %dy_ref.1, bf16[1536,6144]{1,0:T(8,128)(2,1)} %w_in.1, ...), custom_call_target="tpu_custom_call" | custom-call | flops 19327352832 | bytes 75497472 | tf_op jit(solution)/shard_map/middle/pallas_call | solution.py:329
  129.8 0.0 slice-start
  129.8 0.0 reduce-scatter.2.cloned.1.call-update
  129.9 0.0 slice-start.1
  129.9 0.0 copy-start
  129.9 16.5 %convolution_convert_fusion = bf16[1536,6144]{1,0:T(8,128)(2,1)} fusion(bf16[512,1536]{1,0:T(8,128)(2,1)} %bitcast.13, bf16[512,6144]{1,0:T(8,128)(2,1)} %bitcast.11), kind=kOutput, calls=%fused_computation | convolution fusion | flops 9673113600 | bytes 26738688 | tf_op jit(solution)/shard_map/dot_general | solution.py:19
  146.4 0.0 slice-done
  146.4 0.0 slice-done.1
  146.4 0.0 copy-done
  146.4 13.2 %convolution_convert_fusion.1 = bf16[6144,1536]{1,0:T(8,128)(2,1)} fusion(bf16[512,6144]{1,0:T(8,128)(2,1)S(1)} %bitcast.10, bf16[512,1536]{1,0:T(8,128)(2,1)S(1)} %bitcast.12), kind=kOutput, calls=%fused_computation.1 | convolution fusion | flops 9673113600 | bytes 26738688 | tf_op jit(solution)/shard_map/dot_general | solution.py:19
  159.6 8.2 %reduce-scatter.2.cloned.1.call-done = bf16[64,3072]{1,0:T(8,128)(2,1)} async-done(((bf16[256,3072]{1,0:T(8,128)(2,1)}), bf16[64,3072]{1,0:T(8,128)(2,1)}) %reduce-scatter.2.cloned.1.call-update) | async-done | bytes 393232 | tf_op jit(solution)/shard_map/reduce_scatter | solution.py:381
  167.8 1.8 %fusion = (bf16[64,1536]{1,0:T(8,128)(2,1)}, bf16[64,1536]{1,0:T(8,128)(2,1)}) fusion(bf16[64,3072]{1,0:T(8,128)(2,1)} %reduce-scatter.2.cloned.1.call-done), kind=kLoop, calls=%fused_computation.2 | loop fusion | bytes 786432 | tf_op jit(solution)/shard_map/slice | solution.py:382
  (1 shorter events, 0.0 us)
Async XLA Ops:
  7.2 160.7 %reduce-scatter.2.cloned.1.call-start = ((), (), s32[]{:S(2)}) async-start(), calls=%async_computation.1 | async-start | bytes 1966080 | tf_op jit(solution)/shard_map/reduce_scatter | solution.py:381
  129.8 16.6 %slice-start = ((s8[6291456]{0:T(1024)(128)(4,1)}), s8[2097152]{0:T(1024)(128)(4,1)S(1)}, s32[]{:S(2)}) async-start(s8[6291456]{0:T(1024)(128)(4,1)} %bitcast.8), calls=%async_computation.2 | async-start | bytes 4194304
  129.9 16.5 %slice-start.1 = ((s8[6291456]{0:T(1024)(128)(4,1)}), s8[4194304]{0:T(1024)(128)(4,1)S(1)}, s32[]{:S(2)}) async-start(s8[6291456]{0:T(1024)(128)(4,1)} %bitcast.8), calls=%async_computation.3 | async-start | bytes 8388608
  129.9 16.5 %copy-start = (bf16[2,4,64,1536]{3,2,1,0:T(8,128)(2,1)S(1)}, bf16[2,4,64,1536]{3,2,1,0:T(8,128)(2,1)}, u32[]{:S(2)}) copy-start(bf16[2,4,64,1536]{3,2,1,0:T(8,128)(2,1)} %get-tuple-element.13) | copy-start | bytes 4718596
Sparse Core Ops, SparseCore 0:
  130.0 37.7 reduce-scatter.1

commit v4 on v3

--- a/solution.py
+++ b/solution.py
@@ -94,8 +94,7 @@
             pltpu.make_async_copy(w_out.at[cols, :], we_out.at[slot], we_sem.at[slot, 1]),
         )
 
-    for copy in load_a(0, 0):
-        copy.start()
+    load_a(0, 0)[0].start()
     own = [
         pltpu.make_async_copy(ref, xg.at[a, me_dp, me_col], x_local.at[a])
         for a, ref in enumerate((x_ref, dy_ref))
@@ -113,9 +112,8 @@
             {"col": col_peer(d)},
         )
 
-    for a in range(2):
-        for d in range(1, n_col):
-            x_copy(a, d, me_col).start()
+    for d in range(1, n_col):
+        x_copy(0, d, me_col).start()
     for copy in own:
         copy.wait()
 
@@ -125,10 +123,14 @@
 
     for a in range(2):
         d_copy(a, me_dp, 0).start()
-    for a in range(2):
+    def arrive(a):
         for d in range(1, n_col):
             x_copy(a, d, col_from(d)).wait_recv()
             d_copy(a, me_dp, d).start()
+
+    arrive(0)
+    for d in range(1, n_col):
+        x_copy(1, d, me_col).start()
 
     def core_copy(c, k):
         return remote(parts.at[c, k], crecv.at[c], c_ssem.at[c], c_rsem.at[c], to_core)
@@ -140,7 +142,7 @@
         )
 
     def piece(c, dp, y, k):
-        return gat.at[c, :, dp, y, k]
+        return gat.at[c, dp, y, k]
 
     def share_copy(c, dp, y, k, ssem, peer):
         ref = piece(c, dp, y, k)
@@ -155,69 +157,92 @@
     def ag_c_copy(c, dp, y, k):
         return share_copy(c, dp, y, k, ag_c.at[c, dp, y], to_core)
 
-    def out_copy(c, a):
+    def out_copy(v, a):
+        c = v - a * chunks
         cols = pl.ds(pl.multiple_of(c * width, width), width)
         return pltpu.make_async_copy(
-            gat.at[c, a], (hid_all, gp_all)[a].at[:, :, :, :, cols], o_sem.at[c, a]
+            gat.at[v], (hid_all, gp_all)[a].at[:, :, :, :, cols], o_sem.at[v]
         )
 
     n_tile = tile_of(width, 256)
     d_tile = tile_of(depth, 256)
 
+    def each(v, body):
+        for a in range(2):
+            @pl.when(jnp.logical_and(v >= a * chunks, v < (a + 1) * chunks))
+            def _(a=a):
+                body(a)
+
+    def fetch(load, v, which):
+        def body(a):
+            c = v - a * chunks
+            load(c, lax.rem(c, 2))[which(a)].start()
+
+        each(v, body)
+
     def stage_a(c):
-        slot = lax.rem(c, 2)
-
-        @pl.when(c + 1 < chunks)
-        def _():
-            for copy in load_a(c + 1, 1 - slot):
-                copy.start()
-
-        for copy in load_a(c, slot):
-            copy.wait()
-        x = xg[0, me_dp].reshape(group, depth)
-        dy = xg[1, me_dp].reshape(group, depth)
-        for t in range(width // n_tile):
-            cols = slice(t * n_tile, (t + 1) * n_tile)
-            pre = jnp.dot(x, wa_in[slot, :, cols], preferred_element_type=F32)
-            grad = contract_cols(dy, wa_out[slot, cols, :])
-            for a, part in enumerate((pre, grad)):
+        fetch(load_a, c + 1, lambda a: a)
+
+        def body(a):
+            if a == 1:
+                @pl.when(c == chunks)
+                def _():
+                    arrive(1)
+
+            slot = lax.rem(c - a * chunks, 2)
+            load_a(c - a * chunks, slot)[a].wait()
+            rows_in = xg[a, me_dp].reshape(group, depth)
+            for t in range(width // n_tile):
+                cols = slice(t * n_tile, (t + 1) * n_tile)
+                if a == 0:
+                    part = jnp.dot(
+                        rows_in, wa_in[slot, :, cols], preferred_element_type=F32
+                    )
+                else:
+                    part = contract_cols(rows_in, wa_out[slot, cols, :])
                 part = part.astype(BF16)
                 for r in range(2 * n_y):
-                    parts[c, r % 2, a, r // 2, :, cols] = part[r * share:(r + 1) * share]
+                    parts[c, r % 2, r // 2, :, cols] = part[r * share:(r + 1) * share]
+
+        each(c, body)
         core_copy(c, other_k).start()
 
     def stage_b(c):
         core_copy(c, me_k).wait_recv()
         for d in range(1, n_y):
             y = y_peer(d)
-            for a in range(2):
-                ysend[c, d - 1, a] = (
-                    parts[c, me_k, a, y].astype(F32) + crecv[c, a, y].astype(F32)
-                ).astype(BF16)
+            ysend[c, d - 1] = (
+                parts[c, me_k, y].astype(F32) + crecv[c, y].astype(F32)
+            ).astype(BF16)
             y_copy(c, d).start()
 
     def stage_c(c):
         for d in range(1, n_y):
             y_copy(c, d).wait_recv()
-        for t in range(width // n_tile):
-            cols = slice(t * n_tile, (t + 1) * n_tile)
-
-            def total(a):
-                value = parts[c, me_k, a, me_y, :, cols].astype(F32)
-                value = value + crecv[c, a, me_y, :, cols].astype(F32)
-                for d in range(1, n_y):
-                    value = value + yrecv[c, d - 1, a, :, cols].astype(F32)
-                return value
-
-            pre, grad = total(0), total(1)
-            square = pre * pre
-            bend = jnp.tanh(SCALE * (pre + CUBIC * (square * pre)))
-            half = 0.5 * (1.0 + bend)
-            slope = half + (0.5 * pre) * (1.0 - bend * bend) * (
-                SCALE * (1.0 + (3.0 * CUBIC) * square)
-            )
-            gat[c, 0, me_dp, me_y, me_k, :, cols] = (pre * half).astype(BF16)
-            gat[c, 1, me_dp, me_y, me_k, :, cols] = (grad * slope).astype(BF16)
+
+        def total(v, cols):
+            value = parts[v, me_k, me_y, :, cols].astype(F32)
+            value = value + crecv[v, me_y, :, cols].astype(F32)
+            for d in range(1, n_y):
+                value = value + yrecv[v, d - 1, :, cols].astype(F32)
+            return value
+
+        def body(a):
+            for t in range(width // n_tile):
+                cols = slice(t * n_tile, (t + 1) * n_tile)
+                pre = total(c - a * chunks, cols)
+                square = pre * pre
+                bend = jnp.tanh(SCALE * (pre + CUBIC * (square * pre)))
+                half = 0.5 * (1.0 + bend)
+                value = pre * half
+                if a == 1:
+                    slope = half + (0.5 * pre) * (1.0 - bend * bend) * (
+                        SCALE * (1.0 + (3.0 * CUBIC) * square)
+                    )
+                    value = total(c, cols) * slope
+                gat[c, me_dp, me_y, me_k, :, cols] = value.astype(BF16)
+
+        each(c, body)
         for d in range(1, n_y):
             ag_y_copy(c, d, me_y).start()
         ag_x_copy(c, me_dp, me_y).start()
@@ -231,25 +256,24 @@
             ag_x_copy(c, me_dp, y).start()
 
     def stage_e(c):
-        slot = lax.rem(c, 2)
-
-        @pl.when(c + 1 < chunks)
-        def _():
-            for copy in load_e(c + 1, 1 - slot):
-                copy.start()
-
+        fetch(load_e, c + 1, lambda a: 1 - a)
         for y in range(n_y):
             ag_c_copy(c, me_dp, y, other_k).wait_recv()
-        for copy in load_e(c, slot):
-            copy.wait()
-        hidden = gat[c, 0, me_dp].reshape(group, width)
-        grad_pre = gat[c, 1, me_dp].reshape(group, width)
-        for t in range(depth // d_tile):
-            cols = slice(t * d_tile, (t + 1) * d_tile)
-            acc_out[:, cols] += jnp.dot(
-                hidden, we_out[slot, :, cols], preferred_element_type=F32
-            )
-            acc_back[:, cols] += contract_cols(grad_pre, we_in[slot, cols, :])
+
+        def body(a):
+            slot = lax.rem(c - a * chunks, 2)
+            load_e(c - a * chunks, slot)[1 - a].wait()
+            value = gat[c, me_dp].reshape(group, width)
+            for t in range(depth // d_tile):
+                cols = slice(t * d_tile, (t + 1) * d_tile)
+                if a == 0:
+                    acc_out[:, cols] += jnp.dot(
+                        value, we_out[slot, :, cols], preferred_element_type=F32
+                    )
+                else:
+                    acc_back[:, cols] += contract_cols(value, we_in[slot, cols, :])
+
+        each(c, body)
 
     def stage_g(c):
         for y in range(n_y):
@@ -259,29 +283,27 @@
     def stage_f(c):
         for y in range(n_y):
             ag_c_copy(c, other_dp, y, other_k).wait_recv()
-        for a in range(2):
-            out_copy(c, a).start()
+        each(c, lambda a: out_copy(c, a).start())
 
     last = 7
 
     def step(i, carry):
         @pl.when(i == 1)
         def _():
-            for copy in load_e(0, 0):
-                copy.start()
+            load_e(0, 0)[1].start()
 
         stages = (
             (0, stage_a), (1, stage_b), (2, stage_c), (3, stage_d), (4, stage_e),
             (last - 1, stage_g), (last, stage_f),
         )
         for lag, stage in stages:
-            @pl.when(jnp.logical_and(i >= lag, i < chunks + lag))
+            @pl.when(jnp.logical_and(i >= lag, i < 2 * chunks + lag))
             def _(lag=lag, stage=stage):
                 stage(i - lag)
 
         return carry
 
-    lax.fori_loop(0, chunks + last, step, 0)
+    lax.fori_loop(0, 2 * chunks + last, step, 0)
 
     out_ref[:, :depth] = acc_out[...].astype(BF16)
     out_ref[:, depth:] = acc_back[...].astype(BF16)
@@ -306,11 +328,10 @@
             ag_x_copy(c, me_dp, y).wait_send()
             for dp in range(2):
                 ag_c_copy(c, dp, y, me_k).wait_send()
-        for a in range(2):
-            out_copy(c, a).wait()
+        each(c, lambda a: out_copy(c, a).wait())
         return carry
 
-    lax.fori_loop(0, chunks, drain, 0)
+    lax.fori_loop(0, 2 * chunks, drain, 0)
     for copy in x_out:
         copy.wait()
 
@@ -339,11 +360,11 @@
         out_specs=[vmem] + [any_space] * 4,
         scratch_shapes=[
             pltpu.VMEM((2, 2, n_col, rows, depth), BF16),
-            pltpu.VMEM((chunks, 2, 2, n_y, share, width), BF16),
-            pltpu.VMEM((chunks, 2, n_y, share, width), BF16),
-            pltpu.VMEM((chunks, n_y - 1, 2, share, width), BF16),
-            pltpu.VMEM((chunks, n_y - 1, 2, share, width), BF16),
-            pltpu.VMEM((chunks, 2, 2, n_y, 2, share, width), BF16),
+            pltpu.VMEM((2 * chunks, 2, n_y, share, width), BF16),
+            pltpu.VMEM((2 * chunks, n_y, share, width), BF16),
+            pltpu.VMEM((2 * chunks, n_y - 1, share, width), BF16),
+            pltpu.VMEM((2 * chunks, n_y - 1, share, width), BF16),
+            pltpu.VMEM((2 * chunks, 2, n_y, 2, share, width), BF16),
             pltpu.VMEM((2, depth, width), BF16),
             pltpu.VMEM((2, width, depth), BF16),
             pltpu.VMEM((2, depth, width), BF16),
@@ -355,17 +376,17 @@
             dma((2, n_col - 1)),
             dma((2, n_col)),
             dma((2, n_col)),
-            dma((chunks,)),
-            dma((chunks,)),
-            dma((chunks, n_y - 1)),
-            dma((chunks, n_y - 1)),
-            dma((chunks, 2, n_y, 2)),
-            dma((chunks, n_y - 1)),
-            dma((chunks, n_y)),
-            dma((chunks, 2, n_y)),
+            dma((2 * chunks,)),
+            dma((2 * chunks,)),
+            dma((2 * chunks, n_y - 1)),
+            dma((2 * chunks, n_y - 1)),
+            dma((2 * chunks, 2, n_y, 2)),
+            dma((2 * chunks, n_y - 1)),
+            dma((2 * chunks, n_y)),
+            dma((2 * chunks, 2, n_y)),
             dma((2, 2)),
             dma((2, 2)),
-            dma((chunks, 2)),
+            dma((2 * chunks,)),
             dma((2,)),
         ],
         compiler_params=pltpu.CompilerParams(

time: 177 us -> 172 us (0.972)
  Pallas kernels: 123 us -> 116 us
  waiting for transfers between devices: 8.21 us -> 10.4 us
    pallas_call x1, Pallas kernels: 123 us -> 116 us  [shards(): pl.pallas_call(functools.partial(middle, (n_col, n_y, chunks, width)), ou...]
    reduce_scatter x1, waiting for transfers between devices: 8.19 us -> 10.4 us  [shards(): total = lax.psum_scatter(part, 'col', scatter_dimension=0, tiled=True)]
where the time goes in v4:
time: 172 us
  Pallas kernels  116 us (67%)
  matrix products  29.7 us (17%)
  between operations  14.1 us (8%)
  waiting for transfers between devices  10.4 us (6%)
  local copies, waits for them, and re-layouts  1.8 us (1%)
    pallas_call x1, Pallas kernels, shards(): pl.pallas_call(functools.partial(middle, (n_col, n_y, chunks, width)), ou...  116 us
    dot_general x2, matrix products, contract_rows(): lax.dot_general(left, right, (((0,), (0,)), ((), ())), preferred_element_...  29.7 us
    reduce_scatter x1, waiting for transfers between devices, shards(): total = lax.psum_scatter(part, 'col', scatter_dimension=0, tiled=True)  10.4 us
  transfers between devices with their start and end apart: 1, of which 1 were waited for; matrix products, arithmetic and copies ran while one was open for 17% of the time, Pallas kernels for 0%

profile of v4, /device:TPU:0, one launch (start us, length us, event | category | flops | bytes accessed | tf_op | source)
XLA Modules:
  0.0 172.2 jit_solution(4788909087037496594)
XLA Ops:
  7.2 0.0 reduce-scatter.2.cloned.1.call-start
  7.2 116.1 %middle.1 = (bf16[256,3072]{1,0:T(8,128)(2,1)}, bf16[2,2,2,64,6144]{4,3,2,1,0:T(8,128)(2,1)}, bf16[2,2,2,64,6144]{4,3,2,1,0:T(8,128)(2,1)}, bf16[2,4,64,1536]{3,2,1,0:T(8,128)(2,1)}, bf16[2,4,64,1536]{3,2,1,0:T(8,128)(2,1)}) custom-call(bf16[64,1536]{1,0:T(8,128)(2,1)} %x_ref.1, bf16[64,1536]{1,0:T(8,128)(2,1)} %dy_ref.1, bf16[1536,6144]{1,0:T(8,128)(2,1)} %w_in.1, ...), custom_call_target="tpu_custom_call" | custom-call | flops 19327352832 | bytes 75497472 | tf_op jit(solution)/shard_map/middle/pallas_call | solution.py:350
  123.4 0.0 slice-start
  123.4 0.0 reduce-scatter.2.cloned.1.call-update
  123.4 0.0 slice-start.1
  123.4 0.0 copy-start
  123.4 16.5 %convolution_convert_fusion = bf16[1536,6144]{1,0:T(8,128)(2,1)} fusion(bf16[512,1536]{1,0:T(8,128)(2,1)} %bitcast.13, bf16[512,6144]{1,0:T(8,128)(2,1)} %bitcast.11), kind=kOutput, calls=%fused_computation | convolution fusion | flops 9673113600 | bytes 26738688 | tf_op jit(solution)/shard_map/dot_general | solution.py:19
  139.9 0.0 slice-done
  139.9 0.0 slice-done.1
  139.9 0.0 copy-done
  139.9 13.2 %convolution_convert_fusion.1 = bf16[6144,1536]{1,0:T(8,128)(2,1)} fusion(bf16[512,6144]{1,0:T(8,128)(2,1)S(1)} %bitcast.10, bf16[512,1536]{1,0:T(8,128)(2,1)S(1)} %bitcast.12), kind=kOutput, calls=%fused_computation.1 | convolution fusion | flops 9673113600 | bytes 26738688 | tf_op jit(solution)/shard_map/dot_general | solution.py:19
  153.2 10.4 %reduce-scatter.2.cloned.1.call-done = bf16[64,3072]{1,0:T(8,128)(2,1)} async-done(((bf16[256,3072]{1,0:T(8,128)(2,1)}), bf16[64,3072]{1,0:T(8,128)(2,1)}) %reduce-scatter.2.cloned.1.call-update) | async-done | bytes 393232 | tf_op jit(solution)/shard_map/reduce_scatter | solution.py:402
  163.6 1.8 %fusion = (bf16[64,1536]{1,0:T(8,128)(2,1)}, bf16[64,1536]{1,0:T(8,128)(2,1)}) fusion(bf16[64,3072]{1,0:T(8,128)(2,1)} %reduce-scatter.2.cloned.1.call-done), kind=kLoop, calls=%fused_computation.2 | loop fusion | bytes 786432 | tf_op jit(solution)/shard_map/slice | solution.py:403
  (1 shorter events, 0.0 us)
Async XLA Ops:
  7.2 156.4 %reduce-scatter.2.cloned.1.call-start = ((), (), s32[]{:S(2)}) async-start(), calls=%async_computation.1 | async-start | bytes 1966080 | tf_op jit(solution)/shard_map/reduce_scatter | solution.py:402
  123.4 16.6 %slice-start = ((s8[6291456]{0:T(1024)(128)(4,1)}), s8[2097152]{0:T(1024)(128)(4,1)S(1)}, s32[]{:S(2)}) async-start(s8[6291456]{0:T(1024)(128)(4,1)} %bitcast.8), calls=%async_computation.2 | async-start | bytes 4194304
  123.4 16.5 %slice-start.1 = ((s8[6291456]{0:T(1024)(128)(4,1)}), s8[4194304]{0:T(1024)(128)(4,1)S(1)}, s32[]{:S(2)}) async-start(s8[6291456]{0:T(1024)(128)(4,1)} %bitcast.8), calls=%async_computation.3 | async-start | bytes 8388608
  123.4 16.5 %copy-start = (bf16[2,4,64,1536]{3,2,1,0:T(8,128)(2,1)S(1)}, bf16[2,4,64,1536]{3,2,1,0:T(8,128)(2,1)}, u32[]{:S(2)}) copy-start(bf16[2,4,64,1536]{3,2,1,0:T(8,128)(2,1)} %get-tuple-element.13) | copy-start | bytes 4718596
Sparse Core Ops, SparseCore 0:
  123.5 40.0 reduce-scatter.1
